TPU v7x, 32 devices: a whole 2x2x4 slice. The times are simulated.
32 devices in a mesh: tm: 4 (over y, x), video: 8 (over z, core).
Axes of the slice: x: 2, y: 2, z: 4, core: 2. Of those that a mesh axis runs over, the one named last changes fastest.
Arguments:
- latent: bfloat16 [4, 3, 4, 12, 128, 16], P('tm', None, None, None, 'video'), may hold values from -6 to 6
- routing: int32 [4], replicated, may hold values from 0 to 3, each once
- counts: int32 [4], replicated, may hold values from 1 to 4, as said below
- offsets: int32 [4], replicated, may hold values from 0 to 3, as said below
- in_weight: bfloat16 [3, 3, 48, 384], replicated, may hold values from -0.3125 to 0.3125
- in_bias: float32 [384], replicated, may hold values from -3 to 3
- first_gain: float32 [384], replicated, may hold values from 0.1 to 1.9
- first_weight: bfloat16 [3, 3, 1152, 384], replicated, may hold values from -0.0625 to 0.0625
- first_bias: float32 [384], replicated, may hold values from -3 to 3
- second_gain: float32 [384], replicated, may hold values from 0.1 to 1.9
- second_weight: bfloat16 [3, 3, 1152, 384], replicated, may hold values from -0.0625 to 0.0625
- second_bias: float32 [384], replicated, may hold values from -3 to 3
Outputs:
- decoded: bfloat16 [4, 3, 48, 128, 384], P('tm', None, 'video')
Inputs may be any that keep to these rules, and one draw needn't show every extreme that they name: `routing`: a permutation: each video has its own decoder slot. `counts`: every video has at least one span. offsets[v] + counts[v] <= 4.
All inputs are finite; a program needn't handle non-finite values.
Results may differ from a plain program's by a relative error of at most 0.013.
Values may be sent and summed in bfloat16 or wider, within the bound.
A program may use at most 384 MiB of HBM per device.

v0:
```python
import functools

import jax
import jax.numpy as jnp
from jax import lax
from jax.experimental import pallas as pl
from jax.experimental.pallas import tpu as pltpu
from jax.sharding import PartitionSpec as P

BANDS = 4
VPG = 2
F32 = jnp.float32
BF16 = jnp.bfloat16
LIMIT = 58 * 1024 * 1024


def weight_copies(weight_ref, held, sems):
    width = weight_ref.shape[-1]
    return [
        pltpu.make_async_copy(
            weight_ref.at[i, j], held.at[j, :, pl.ds(i * width, width)], sems.at[i, j]
        )
        for j in range(3)
        for i in range(3)
    ]


def spread_columns(values, cols):
    rows = values.shape[0]
    place = lax.broadcasted_iota(jnp.int32, values.shape, 0) % cols
    left = jnp.where(place == 0, 0.0, pltpu.roll(values, 1, 0))
    right = jnp.where(place == cols - 1, 0.0, pltpu.roll(values, rows - 1, 0))
    return jnp.concatenate(
        [left.astype(BF16), values.astype(BF16), right.astype(BF16)], axis=-1
    )


def norm_silu(values, gain):
    scale = lax.rsqrt(jnp.mean(values * values, axis=-1, keepdims=True) + 1e-06)
    half = (0.5 * gain) * (values * scale)
    return half + half * jnp.tanh(half)


def accumulate(acc, x, w):
    width = acc.shape[-1]
    rows = acc.shape[1]
    frames = acc.shape[0]

    def step(j, carry):
        for a in range(frames + 2):
            low, high = max(0, a - frames + 1), min(2, a)
            lhs = x[a, pl.ds(j, 3)].reshape(rows, 3 * width)
            res = jnp.dot(
                lhs, w[j, :, low * width : (high + 1) * width], preferred_element_type=F32
            )
            for i in range(low, high + 1):
                acc[a - i] += res[:, (i - low) * width : (i - low + 1) * width]
        return carry

    lax.fori_loop(0, 3, step, 0)


def video_scale(mask_ref, frame, half):
    place = lax.broadcasted_iota(jnp.int32, (half * VPG, 1), 0)
    return jnp.where(place < half, mask_ref[frame, 0], mask_ref[frame, 1])


def front_kernel(
    live_ref, keep_ref, lat_ref, in_w_ref, in_b_ref, gain1_ref, b1_ref, gain2_ref, w1_ref,
    hidden_ref, second_ref, x, w, acc, sems,
):
    width = in_w_ref.shape[-1]
    lanes = lat_ref.shape[-1]
    cols = lanes // VPG
    copies = weight_copies(w1_ref, w, sems)
    for copy in copies:
        copy.start()
    frames, rows = x.shape[0], x.shape[1]

    def cell(index, carry):
        f, r = index // rows, index % rows
        taps = jnp.concatenate(
            [lat_ref[f + i, r + j] for i in range(3) for j in range(3)], axis=0
        )
        value = lax.dot_general(
            taps, in_w_ref[...], (((0,), (0,)), ((), ())), preferred_element_type=F32
        )
        scale = video_scale(live_ref, f, cols) * keep_ref[r]
        value = ((value + in_b_ref[...]) * scale).astype(BF16)
        hidden_ref[f, r] = value
        x[f, r] = spread_columns(norm_silu(value.astype(F32), gain1_ref[...]), cols)
        return carry

    lax.fori_loop(0, frames * rows, cell, 0)
    for o in range(acc.shape[0]):
        acc[o] = jnp.broadcast_to(b1_ref[...], acc.shape[1:])
    for copy in copies:
        copy.wait()
    accumulate(acc, x, w)

    def finish(index, carry):
        f, r = index // (rows - 2), index % (rows - 2)
        value = acc[f, pl.ds(pl.multiple_of(r * lanes, lanes), lanes)]
        value = value * video_scale(live_ref, f + 2, cols)
        second_ref[f, r] = norm_silu(value, gain2_ref[...]).astype(BF16)
        return carry

    lax.fori_loop(0, acc.shape[0] * (rows - 2), finish, 0)


def back_kernel(
    live_ref, keep_ref, own_ref, behind_ref, above_ref, below_ref, hidden_ref, b2_ref, w2_ref,
    out_ref, x, w, acc, sems,
):
    frames, rows, lanes, width = own_ref.shape
    cols = lanes // VPG
    copies = weight_copies(w2_ref, w, sems)
    for copy in copies:
        copy.start()

    def fill_own(index, carry):
        f, r = index // rows, index % rows
        x[f + 2, r + 1] = spread_columns(own_ref[f, r].astype(F32), cols)
        return carry

    lax.fori_loop(0, frames * rows, fill_own, 0)

    def fill_behind(index, carry):
        f, r = index // rows, index % rows
        x[f, r + 1] = spread_columns(behind_ref[f, r].astype(F32), cols)
        return carry

    lax.fori_loop(0, 2 * rows, fill_behind, 0)

    def fill_rows(f, carry):
        x[f, 0] = spread_columns(above_ref[f].astype(F32) * keep_ref[0], cols)
        x[f, rows + 1] = spread_columns(below_ref[f].astype(F32) * keep_ref[rows + 1], cols)
        return carry

    lax.fori_loop(0, frames + 2, fill_rows, 0)
    for o in range(frames):
        acc[o] = jnp.broadcast_to(b2_ref[...], acc.shape[1:])
    for copy in copies:
        copy.wait()
    accumulate(acc, x, w)

    for f in range(frames):
        for r in range(rows):
            value = acc[f, r * lanes : (r + 1) * lanes] + hidden_ref[f + 2, r + 1].astype(F32)
            value = (value * video_scale(live_ref, f + 2, cols)).astype(BF16)
            for v in range(VPG):
                out_ref[f, v * rows + r] = value[v * cols : (v + 1) * cols]


def on_device(
    latent, routing, counts, offsets, in_weight, in_bias, first_gain, first_weight, first_bias,
    second_gain, second_weight, second_bias,
):
    groups = lax.axis_size("video")
    spans = lax.axis_size("tm")
    group_count = groups // BANDS
    _, frames, videos, window_rows, local_cols, z = latent.shape
    rows = window_rows // BANDS
    width = in_weight.shape[-1]
    cols = local_cols * groups
    lanes = VPG * cols
    device_index = lax.axis_index("video")
    placed = (device_index + BANDS // 2) % groups
    group, band = placed // BANDS, placed % BANDS
    span = lax.axis_index("tm")

    slots = jnp.arange(videos, dtype=jnp.int32)
    chosen = routing[:, None] == slots[None, :]
    video_of = jnp.sum(jnp.where(chosen, slots[:, None], 0), axis=0)
    first_span = jnp.sum(jnp.where(chosen, offsets[:, None], 0), axis=0)
    last_span = first_span + jnp.sum(jnp.where(chosen, counts[:, None], 0), axis=0)
    first_own = lax.dynamic_slice_in_dim(first_span, group * VPG, VPG)
    last_own = lax.dynamic_slice_in_dim(last_span, group * VPG, VPG)
    relative = jnp.arange(frames + 4, dtype=jnp.int32) - 4
    span_of = span + jnp.floor_divide(relative, frames)
    live = ((span_of[:, None] >= first_own) & (span_of[:, None] < last_own)).astype(F32)
    row_ids = band * rows - 1 + jnp.arange(rows + 2, dtype=jnp.int32)
    keep = ((row_ids >= 0) & (row_ids < window_rows)).astype(F32)

    own = jnp.take(latent[0], video_of, axis=1)
    one = lax.ppermute(own, "tm", [(i, i + 1) for i in range(spans - 1)])
    two = lax.ppermute(own[-1:], "tm", [(i, i + 2) for i in range(spans - 2)])
    line = jnp.concatenate([two, one, own], axis=0)
    line = jnp.pad(line, ((0, 0), (0, 0), (2, 2), (0, 0), (0, 0)))
    bands = jnp.stack(
        [line[:, :, b * rows : b * rows + rows + 4] for b in range(BANDS)], axis=0
    )
    bands = bands.reshape(BANDS, frames + 4, group_count, VPG, rows + 4, local_cols, z)
    bands = jnp.transpose(bands, (2, 0, 1, 4, 3, 6, 5))
    bands = bands.reshape(groups, frames + 4, rows + 4, VPG, z, local_cols)
    bands = jnp.roll(bands, -(BANDS // 2), axis=0)
    came = lax.all_to_all(bands, "video", split_axis=0, concat_axis=0, tiled=True)
    came = jnp.transpose(came, (1, 2, 4, 3, 0, 5)).reshape(frames + 4, rows + 4, z, VPG, cols)
    came = (came * live[:, None, None, :, None]).astype(BF16)
    wide = jnp.pad(came, ((0, 0),) * 4 + ((1, 1),))
    stacked = jnp.stack([wide[..., k : k + cols] for k in range(3)], axis=2)
    stacked = stacked.reshape(frames + 4, rows + 4, 3 * z, lanes)

    vmem = pl.BlockSpec(memory_space=pltpu.VMEM)
    smem = pl.BlockSpec(memory_space=pltpu.SMEM)
    hbm = pl.BlockSpec(memory_space=pl.ANY)
    scratch = [
        pltpu.VMEM((frames + 2, rows + 2, lanes, 3 * width), BF16),
        pltpu.VMEM((3, 3 * width, 3 * width), BF16),
        pltpu.VMEM((frames, rows * lanes, width), F32),
        pltpu.SemaphoreType.DMA((3, 3)),
    ]
    params = pltpu.CompilerParams(vmem_limit_bytes=LIMIT)
    live5 = live[2:]
    hidden, second = pl.pallas_call(
        front_kernel,
        out_shape=(
            jax.ShapeDtypeStruct((frames + 2, rows + 2, lanes, width), BF16),
            jax.ShapeDtypeStruct((frames, rows, lanes, width), BF16),
        ),
        in_specs=[smem, smem] + [vmem] * 6 + [hbm],
        out_specs=(vmem, vmem),
        scratch_shapes=scratch,
        compiler_params=params,
    )(
        live5, keep, stacked, in_weight.reshape(9 * 3 * z, width), in_bias[None],
        first_gain[None], first_bias[None], second_gain[None], first_weight,
    )

    behind = lax.ppermute(second[-2:], "tm", [(i, i + 1) for i in range(spans - 1)])
    tall = jnp.concatenate([behind[:, 0::rows - 1], second[:, 0::rows - 1]], axis=0)
    above = lax.ppermute(
        tall[:, 1], "video", [(i, (i + 1) % groups) for i in range(groups)]
    )
    below = lax.ppermute(
        tall[:, 0], "video", [((i + 1) % groups, i) for i in range(groups)]
    )
    out = pl.pallas_call(
        back_kernel,
        out_shape=jax.ShapeDtypeStruct((frames, VPG * rows, cols, width), BF16),
        in_specs=[smem, smem] + [vmem] * 6 + [hbm],
        out_specs=vmem,
        scratch_shapes=scratch,
        compiler_params=params,
    )(live5, keep, second, behind, above, below, hidden, second_bias[None], second_weight)
    return out[None]


def solution(mesh):
    in_specs = (P("tm", None, None, None, "video", None),) + (P(),) * 11
    return jax.shard_map(
        on_device,
        mesh=mesh,
        in_specs=in_specs,
        out_specs=P("tm", None, "video", None, None),
        check_vma=False,
    )
```

profile of v0, /device:TPU:4, one launch (start us, length us, event | category | flops | bytes accessed | tf_op | source)
XLA Modules:
  0.0 223.4 jit_solution(5832224199322382669)
XLA Ops:
  0.0 0.8 select_reduce_fusion
  0.9 0.2 copy-done
  1.1 0.7 gather_fusion
  1.9 3.4 %collective-permute-start.1 = (bf16[3,4,12,16,16]{4,3,2,0,1:T(8,128)(2,1)S(1)}, bf16[3,4,12,16,16]{4,3,2,0,1:T(8,128)(2,1)S(1)}, u32[]{:S(2)}, u32[]{:S(2)}) collective-permute-start(bf16[3,4,12,16,16]{4,3,2,0,1:T(8,128)(2,1)S(1)} %select_bitcast_fusion), channel_id=1, source_target_pairs={{0,8},{8,16},{16,24},{1,9},{9,17},{17,25},{2,10},{10,18},{18,26},{... | collective-permute-start | bytes 221192 | tf_op jit(solution)/shard_map/ppermute | solution.py:186
  5.3 1.3 collective-permute-start
  6.6 17.3 %collective-permute-done = bf16[1,4,12,16,16]{4,3,2,0,1:T(8,128)(2,1)S(1)} collective-permute-done((bf16[1,4,12,16,16]{4,3,2,0,1:T(8,128)(2,1)S(1)}, bf16[1,4,12,16,16]{4,3,2,0,1:T(8,128)(2,1)S(1)}, u32[]{:S(2)}, u32[]{:S(2)}) %collective-permute-start) | collective-permute-done | bytes 24608 | tf_op jit(solution)/shard_map/ppermute | solution.py:187
  24.0 0.3 pad_maximum_fusion.1
  24.3 0.5 pad_slice_fusion.3
  24.8 0.2 copy.39
  25.0 0.2 copy.40
  25.2 0.2 copy.41
  25.3 0.2 copy.42
  25.5 2.1 maximum_bitcast_fusion
  27.6 5.7 %copy.43 = bf16[2,4,7,7,2,16,16]{6,5,4,3,2,1,0:T(8,128)(2,1)} copy(bf16[2,4,7,7,2,16,16]{5,6,3,4,0,2,1:T(8,128)(2,1)} %maximum_bitcast_fusion) | data formatting | bytes 802816 | tf_op jit(solution)/shard_map/transpose | solution.py:194
  33.4 2.1 slice.70
  35.5 1.2 slice.71
  36.7 2.3 %pad_maximum_fusion = bf16[8,7,7,2,16,16]{5,4,3,2,1,0:T(8,128)(2,1)} fusion(bf16[2,7,7,2,16,16]{5,4,3,2,1,0:T(8,128)(2,1)S(1)} %slice.71, bf16[6,7,7,2,16,16]{5,4,3,2,1,0:T(8,128)(2,1)S(1)} %slice.70), kind=kLoop, calls=%fused_computation.3 | loop fusion | flops 200704 | bytes 802816 | tf_op jit(solution)/shard_map/jit(_roll_static)/concatenate | solution.py:196
  39.0 5.5 %reshape.138 = bf16[8,2,12544]{2,1,0:T(2,128)(2,1)} reshape(bf16[8,7,7,2,16,16]{5,4,3,2,1,0:T(8,128)(2,1)} %pad_maximum_fusion) | data formatting | bytes 802816
  44.5 4.9 %all-to-all-start = ((bf16[8,2,12544]{2,1,0:T(2,128)(2,1)}), bf16[8,2,12544]{2,1,0:T(2,128)(2,1)S(1)}, u32[]{:S(2)}, u32[]{:S(2)}) async-start(bf16[8,2,12544]{2,1,0:T(2,128)(2,1)} %reshape.138), calls=%async_computation | async-start | bytes 802816 | tf_op jit(solution)/shard_map/all_to_all | solution.py:197
  49.6 0.6 slice.50.live_ref
  50.2 0.5 broadcast_in_dim.68.in_b_ref
  50.7 0.6 broadcast_in_dim.69.gain1_ref
  51.3 0.6 broadcast_in_dim.70.b1_ref
  51.9 0.6 broadcast_in_dim.71.gain2_ref
  52.5 0.5 and_convert_fusion.1.keep_ref
  53.0 9.1 %all-to-all-done = bf16[8,2,12544]{2,1,0:T(2,128)(2,1)S(1)} async-done(((bf16[8,2,12544]{2,1,0:T(2,128)(2,1)}), bf16[8,2,12544]{2,1,0:T(2,128)(2,1)S(1)}, u32[]{:S(2)}, u32[]{:S(2)}) %all-to-all-start) | async-done | bytes 401440 | tf_op jit(solution)/shard_map/all_to_all | solution.py:197
  62.1 3.5 %reshape.139 = bf16[8,7,7,2,16,16]{5,4,3,2,1,0:T(8,128)(2,1)} reshape(bf16[8,2,12544]{2,1,0:T(2,128)(2,1)S(1)} %all-to-all-done) | data formatting | bytes 802816
  65.5 2.8 %convert_bitcast_fusion = f32[7,7,16,2,8,16]{5,2,3,1,0,4:T(8,128)S(1)} fusion(bf16[8,7,7,2,16,16]{5,4,3,2,1,0:T(8,128)(2,1)} %reshape.139), kind=kLoop, calls=%fused_computation.1 | loop fusion | flops 200704 | bytes 1204224 | tf_op jit(solution)/shard_map/convert_element_type | solution.py:199
  68.3 8.8 %copy.44 = f32[7,7,16,2,8,16]{5,4,2,3,1,0:T(8,128)} copy(f32[7,7,16,2,8,16]{5,2,3,1,0,4:T(8,128)S(1)} %convert_bitcast_fusion) | data formatting | bytes 1605632 | tf_op jit(solution)/shard_map/convert_element_type | solution.py:199
  77.1 4.3 %reshape.128 = f32[7,7,16,2,128]{4,2,3,1,0:T(8,128)S(1)} reshape(f32[7,7,16,2,8,16]{5,4,2,3,1,0:T(8,128)} %copy.44) | data formatting | bytes 1605632 | tf_op jit(solution)/shard_map/convert_element_type | solution.py:199
  81.5 4.3 %reshape.129 = f32[7,7,1,16,2,128]{5,3,4,1,0,2:T(8,128)S(1)} reshape(f32[7,7,16,2,8,16]{5,4,2,3,1,0:T(8,128)} %copy.44) | data formatting | bytes 1605632 | tf_op jit(solution)/shard_map/convert_element_type | solution.py:199
  85.8 0.1 multiply_convert_fusion.1
  86.0 0.3 fusion.3
  86.4 0.1 pad_maximum_fusion.2
  86.5 1.1 copy.46
  87.6 1.6 reshape.126.lat_ref
  89.2 42.6 %shard_map.118 = (bf16[5,5,256,384]{3,2,1,0:T(8,128)(2,1)}, bf16[3,3,256,384]{3,2,1,0:T(8,128)(2,1)}) custom-call(f32[5,2]{1,0:T(8,128)} %slice.50.live_ref, f32[5]{0:T(128)} %and_convert_fusion.1.keep_ref, bf16[7,7,48,256]{3,2,1,0:T(8,128)(2,1)} %reshape.126.lat_ref, bf16[432,384]{1,0:T(8,128)(2,1)} %bitcast.41, f32[1,384]{1,0:T(1,128)} %broadcast_in_dim.68.in_b_ref, ...), custom_call_target="tpu_custom_call" | custom-call | tf_op jit(solution)/shard_map/pallas_call | solution.py:215
  131.8 1.7 copy.47
  133.6 1.9 collective-permute-start.2
  135.7 28.2 %collective-permute-done.2 = bf16[2,3,256,384]{3,2,0,1:T(8,128)(2,1)S(1)} collective-permute-done((bf16[2,3,256,384]{3,2,0,1:T(8,128)(2,1)S(1)}, bf16[2,3,256,384]{3,2,0,1:T(8,128)(2,1)S(1)}, u32[]{:S(2)}, u32[]{:S(2)}) %collective-permute-start.2) | collective-permute-done | bytes 1179680 | tf_op jit(solution)/shard_map/ppermute | solution.py:230
  164.0 0.2 fusion.2
  164.3 3.5 %collective-permute-start.4 = (bf16[5,256,384]{2,1,0:T(8,128)(2,1)S(1)}, bf16[5,256,384]{2,1,0:T(8,128)(2,1)S(1)}, u32[]{:S(2)}, u32[]{:S(2)}) collective-permute-start(bf16[5,256,384]{2,1,0:T(8,128)(2,1)S(1)} %get-tuple-element.12), channel_id=1, source_target_pairs={{1,0},{2,1},{3,2},{4,3},{5,4},{6,5},{7,6},{0,7},{9,8},{10,9},{11,1... | collective-permute-start | bytes 2949128 | tf_op jit(solution)/shard_map/ppermute | solution.py:235
  167.9 0.5 broadcast_in_dim.72.b2_ref
  168.4 1.2 copy.49.behind_ref
  169.5 20.4 %collective-permute-done.3.above_ref = bf16[5,256,384]{2,1,0:T(8,128)(2,1)S(1)} collective-permute-done((bf16[5,256,384]{2,1,0:T(8,128)(2,1)S(1)}, bf16[5,256,384]{2,1,0:T(8,128)(2,1)S(1)}, u32[]{:S(2)}, u32[]{:S(2)}) %collective-permute-start.3) | collective-permute-done | bytes 983072 | tf_op jit(solution)/shard_map/ppermute | solution.py:232
  190.0 1.0 copy-done.2
  191.0 0.3 copy-done.3
  191.3 31.8 %shard_map.119 = bf16[3,6,128,384]{3,2,1,0:T(8,128)(2,1)} custom-call(f32[5,2]{1,0:T(8,128)} %slice.50.live_ref, f32[5]{0:T(128)} %and_convert_fusion.1.keep_ref, bf16[3,3,256,384]{3,2,1,0:T(8,128)(2,1)} %get-tuple-element.7.own_ref, bf16[2,3,256,384]{3,2,1,0:T(8,128)(2,1)} %copy.49.behind_ref, bf16[5,256,384]{2,1,0:T(8,128)(2,1)} %copy-done.2, ...), custom_call_target="tpu_custom_call" | custom-call | tf_op jit(solution)/shard_map/pallas_call | solution.py:238
  (32 shorter events, 0.9 us)
Async XLA Ops:
  0.0 1.1 copy-start
  1.9 22.1 %collective-permute-start.1 = (bf16[3,4,12,16,16]{4,3,2,0,1:T(8,128)(2,1)S(1)}, bf16[3,4,12,16,16]{4,3,2,0,1:T(8,128)(2,1)S(1)}, u32[]{:S(2)}, u32[]{:S(2)}) collective-permute-start(bf16[3,4,12,16,16]{4,3,2,0,1:T(8,128)(2,1)S(1)} %select_bitcast_fusion), channel_id=1, source_target_pairs={{0,8},{8,16},{16,24},{1,9},{9,17},{17,25},{2,10},{10,18},{18,26},{... | collective-permute-start | bytes 221192 | tf_op jit(solution)/shard_map/ppermute | solution.py:186
  5.3 18.6 %collective-permute-start = (bf16[1,4,12,16,16]{4,3,2,0,1:T(8,128)(2,1)S(1)}, bf16[1,4,12,16,16]{4,3,2,0,1:T(8,128)(2,1)S(1)}, u32[]{:S(2)}, u32[]{:S(2)}) collective-permute-start(bf16[1,4,12,16,16]{4,3,2,0,1:T(8,128)(2,1)S(1)} %slice.67), channel_id=1, source_target_pairs={{0,16},{8,24},{1,17},{9,25},{2,18},{10,26},{3,19},{11,27},{4,20},{... | collective-permute-start | bytes 73736 | tf_op jit(solution)/shard_map/ppermute | solution.py:187
  39.0 11.2 %copy-start.4 = (f32[384]{0:T(512)S(1)}, f32[384]{0:T(512)}, u32[]{:S(2)}) copy-start(f32[384]{0:T(512)} %param.17) | copy-start | bytes 4612
  39.0 11.7 %copy-start.5 = (f32[384]{0:T(512)S(1)}, f32[384]{0:T(512)}, u32[]{:S(2)}) copy-start(f32[384]{0:T(512)} %param.18) | copy-start | bytes 4612
  39.0 12.3 %copy-start.6 = (f32[384]{0:T(512)S(1)}, f32[384]{0:T(512)}, u32[]{:S(2)}) copy-start(f32[384]{0:T(512)} %param.20) | copy-start | bytes 4612
  39.0 12.9 %copy-start.7 = (f32[384]{0:T(512)S(1)}, f32[384]{0:T(512)}, u32[]{:S(2)}) copy-start(f32[384]{0:T(512)} %param.21) | copy-start | bytes 4612
  44.5 17.6 %all-to-all-start = ((bf16[8,2,12544]{2,1,0:T(2,128)(2,1)}), bf16[8,2,12544]{2,1,0:T(2,128)(2,1)S(1)}, u32[]{:S(2)}, u32[]{:S(2)}) async-start(bf16[8,2,12544]{2,1,0:T(2,128)(2,1)} %reshape.138), calls=%async_computation | async-start | bytes 802816 | tf_op jit(solution)/shard_map/all_to_all | solution.py:197
  133.6 30.3 %collective-permute-start.2 = (bf16[2,3,256,384]{3,2,0,1:T(8,128)(2,1)S(1)}, bf16[2,3,256,384]{3,2,0,1:T(8,128)(2,1)S(1)}, u32[]{:S(2)}, u32[]{:S(2)}) collective-permute-start(bf16[2,3,256,384]{3,2,0,1:T(8,128)(2,1)S(1)} %slice.72), channel_id=1, source_target_pairs={{0,8},{8,16},{16,24},{1,9},{9,17},{17,25},{2,10},{10,18},{18,26},{... | collective-permute-start | bytes 3538952 | tf_op jit(solution)/shard_map/ppermute | solution.py:230
  164.0 3.8 %copy-start.8 = (f32[384]{0:T(512)S(1)}, f32[384]{0:T(512)}, u32[]{:S(2)}) copy-start(f32[384]{0:T(512)} %param.23) | copy-start | bytes 4612
  164.3 25.7 %collective-permute-start.3 = (bf16[5,256,384]{2,1,0:T(8,128)(2,1)S(1)}, bf16[5,256,384]{2,1,0:T(8,128)(2,1)S(1)}, u32[]{:S(2)}, u32[]{:S(2)}) collective-permute-start(bf16[5,256,384]{2,1,0:T(8,128)(2,1)S(1)} %get-tuple-element.13), channel_id=1, source_target_pairs={{0,1},{1,2},{2,3},{3,4},{4,5},{5,6},{6,7},{7,0},{8,9},{9,10},{10,1... | collective-permute-start | bytes 2949128 | tf_op jit(solution)/shard_map/ppermute | solution.py:232
  164.3 25.7 %collective-permute-start.4 = (bf16[5,256,384]{2,1,0:T(8,128)(2,1)S(1)}, bf16[5,256,384]{2,1,0:T(8,128)(2,1)S(1)}, u32[]{:S(2)}, u32[]{:S(2)}) collective-permute-start(bf16[5,256,384]{2,1,0:T(8,128)(2,1)S(1)} %get-tuple-element.12), channel_id=1, source_target_pairs={{1,0},{2,1},{3,2},{4,3},{5,4},{6,5},{7,6},{0,7},{9,8},{10,9},{11,1... | collective-permute-start | bytes 2949128 | tf_op jit(solution)/shard_map/ppermute | solution.py:235
  190.0 1.0 copy-start.2
  190.0 1.4 copy-start.3
  191.3 31.9 %copy-start.1 = (bf16[1,3,4,12,16,16]{5,4,3,2,1,0:T(8,128)(2,1)S(1)}, bf16[1,3,4,12,16,16]{5,4,3,2,1,0:T(8,128)(2,1)}, u32[]{:S(2)}) copy-start(bf16[1,3,4,12,16,16]{5,4,3,2,1,0:T(8,128)(2,1)} %param.12) | copy-start | bytes 221188
where the time goes:
time: 224 us; the launch traced here: 223 us
  waiting for transfers between devices  75.1 us (34%)
  Pallas kernels  74.4 us (33%)
  local copies, waits for them, and re-layouts  48.6 us (22%)
  starting transfers between devices  15.1 us (7%)
  other arithmetic  9.76 us (4%)
    pallas_call x1, Pallas kernels, on_device(): pl.pallas_call(front_kernel, out_shape=(jax.ShapeDtypeStruct((frames + 2,...  42.6 us
    pallas_call x1, Pallas kernels, on_device(): pl.pallas_call(back_kernel, out_shape=jax.ShapeDtypeStruct((frames, VPG *...  31.8 us
    ppermute x1, waiting for transfers between devices, on_device(): lax.ppermute(second[-2:], 'tm', [(i, i + 1) for i in range(spans - 1)])  28.2 us
    ppermute x1, waiting for transfers between devices, on_device(): lax.ppermute(tall[:, 1], 'video', [(i, (i + 1) % groups) for i in range(g...  20.4 us
    convert_element_type x3, local copies, waits for them, and re-layouts, on_device(): came = (came * live[:, None, None, :, None]).astype(BF16)  17.5 us
    ppermute x1, waiting for transfers between devices, on_device(): two = lax.ppermute(own[-1:], 'tm', [(i, i + 2) for i in range(spans - 2)])  17.3 us
    unnamed x20, local copies, waits for them, and re-layouts  10.5 us
    all_to_all x1, waiting for transfers between devices, on_device(): lax.all_to_all(bands, 'video', split_axis=0, concat_axis=0, tiled=True)  9.06 us
  transfers between devices with their start and end apart: 6, of which 4 were waited for; matrix products, arithmetic and copies ran while one was open for 2% of the time, Pallas kernels for 0%

commit v1 on v0

--- a/solution.py
+++ b/solution.py
@@ -25,14 +25,17 @@
     ]
 
 
-def spread_columns(values, cols):
-    rows = values.shape[0]
-    place = lax.broadcasted_iota(jnp.int32, values.shape, 0) % cols
-    left = jnp.where(place == 0, 0.0, pltpu.roll(values, 1, 0))
-    right = jnp.where(place == cols - 1, 0.0, pltpu.roll(values, rows - 1, 0))
-    return jnp.concatenate(
-        [left.astype(BF16), values.astype(BF16), right.astype(BF16)], axis=-1
-    )
+def spread_columns(place, values, tile):
+    rows, width = values.shape
+    held = values.astype(BF16)
+    which = lax.broadcasted_iota(jnp.int32, (tile, width), 0)
+    first = pltpu.roll(values[rows - tile :], VPG, 0)
+    last = pltpu.roll(values[:tile], tile - VPG, 0)
+    place[:tile, :width] = jnp.where(which < VPG, 0.0, first).astype(BF16)
+    place[tile:, :width] = held[: rows - tile]
+    place[:, width : 2 * width] = held
+    place[: rows - tile, 2 * width :] = held[tile:]
+    place[rows - tile :, 2 * width :] = jnp.where(which >= tile - VPG, 0.0, last).astype(BF16)
 
 
 def norm_silu(values, gain):
@@ -60,35 +63,47 @@
     lax.fori_loop(0, 3, step, 0)
 
 
-def video_scale(mask_ref, frame, half):
-    place = lax.broadcasted_iota(jnp.int32, (half * VPG, 1), 0)
-    return jnp.where(place < half, mask_ref[frame, 0], mask_ref[frame, 1])
+def video_scale(mask_ref, frame, lanes):
+    place = lax.broadcasted_iota(jnp.int32, (lanes, 1), 0)
+    return jnp.where(place % VPG == 0, mask_ref[frame, 0], mask_ref[frame, 1])
+
+
+def gather_taps(lat_ref, q, z, blocks):
+    tile = lat_ref.shape[2]
+    rows = q.shape[1]
+
+    def frame(f, carry):
+        near = [lat_ref[f, r].astype(F32) for r in range(rows + 2)]
+        for c in range(blocks):
+            cut = [value[:, c * z : c * z + 64] for value in near]
+            blank = jnp.zeros((tile, 64), F32)
+            for r in range(rows):
+                both = jnp.concatenate([cut[r], cut[r + 1], cut[r + 2], blank], axis=1)
+                q[f, r, c * tile : (c + 1) * tile] = both.astype(BF16)
+        return carry
+
+    lax.fori_loop(0, lat_ref.shape[0], frame, 0)
 
 
 def front_kernel(
     live_ref, keep_ref, lat_ref, in_w_ref, in_b_ref, gain1_ref, b1_ref, gain2_ref, w1_ref,
-    hidden_ref, second_ref, x, w, acc, sems,
+    hidden_ref, second_ref, x, w, acc, sems, q, *, z,
 ):
-    width = in_w_ref.shape[-1]
-    lanes = lat_ref.shape[-1]
-    cols = lanes // VPG
     copies = weight_copies(w1_ref, w, sems)
     for copy in copies:
         copy.start()
-    frames, rows = x.shape[0], x.shape[1]
+    frames, rows, lanes = x.shape[:3]
+    tile = lat_ref.shape[2]
+    gather_taps(lat_ref, q, z, lanes // tile)
 
     def cell(index, carry):
         f, r = index // rows, index % rows
-        taps = jnp.concatenate(
-            [lat_ref[f + i, r + j] for i in range(3) for j in range(3)], axis=0
-        )
-        value = lax.dot_general(
-            taps, in_w_ref[...], (((0,), (0,)), ((), ())), preferred_element_type=F32
-        )
-        scale = video_scale(live_ref, f, cols) * keep_ref[r]
+        taps = jnp.concatenate([q[f + i, r] for i in range(3)], axis=1)
+        value = jnp.dot(taps, in_w_ref[...], preferred_element_type=F32)
+        scale = video_scale(live_ref, f, lanes) * keep_ref[r]
         value = ((value + in_b_ref[...]) * scale).astype(BF16)
         hidden_ref[f, r] = value
-        x[f, r] = spread_columns(norm_silu(value.astype(F32), gain1_ref[...]), cols)
+        spread_columns(x.at[f, r], norm_silu(value.astype(F32), gain1_ref[...]), tile)
         return carry
 
     lax.fori_loop(0, frames * rows, cell, 0)
@@ -101,7 +116,7 @@
     def finish(index, carry):
         f, r = index // (rows - 2), index % (rows - 2)
         value = acc[f, pl.ds(pl.multiple_of(r * lanes, lanes), lanes)]
-        value = value * video_scale(live_ref, f + 2, cols)
+        value = value * video_scale(live_ref, f + 2, lanes)
         second_ref[f, r] = norm_silu(value, gain2_ref[...]).astype(BF16)
         return carry
 
@@ -110,31 +125,30 @@
 
 def back_kernel(
     live_ref, keep_ref, own_ref, behind_ref, above_ref, below_ref, hidden_ref, b2_ref, w2_ref,
-    out_ref, x, w, acc, sems,
+    out_ref, x, w, acc, sems, turn, *, tile,
 ):
     frames, rows, lanes, width = own_ref.shape
-    cols = lanes // VPG
     copies = weight_copies(w2_ref, w, sems)
     for copy in copies:
         copy.start()
 
     def fill_own(index, carry):
         f, r = index // rows, index % rows
-        x[f + 2, r + 1] = spread_columns(own_ref[f, r].astype(F32), cols)
+        spread_columns(x.at[f + 2, r + 1], own_ref[f, r].astype(F32), tile)
         return carry
 
     lax.fori_loop(0, frames * rows, fill_own, 0)
 
     def fill_behind(index, carry):
         f, r = index // rows, index % rows
-        x[f, r + 1] = spread_columns(behind_ref[f, r].astype(F32), cols)
+        spread_columns(x.at[f, r + 1], behind_ref[f, r].astype(F32), tile)
         return carry
 
     lax.fori_loop(0, 2 * rows, fill_behind, 0)
 
     def fill_rows(f, carry):
-        x[f, 0] = spread_columns(above_ref[f].astype(F32) * keep_ref[0], cols)
-        x[f, rows + 1] = spread_columns(below_ref[f].astype(F32) * keep_ref[rows + 1], cols)
+        spread_columns(x.at[f, 0], above_ref[f].astype(F32) * keep_ref[0], tile)
+        spread_columns(x.at[f, rows + 1], below_ref[f].astype(F32) * keep_ref[rows + 1], tile)
         return carry
 
     lax.fori_loop(0, frames + 2, fill_rows, 0)
@@ -144,12 +158,22 @@
         copy.wait()
     accumulate(acc, x, w)
 
+    blocks = lanes // tile
+    parts = width // 128
     for f in range(frames):
         for r in range(rows):
             value = acc[f, r * lanes : (r + 1) * lanes] + hidden_ref[f + 2, r + 1].astype(F32)
-            value = (value * video_scale(live_ref, f + 2, cols)).astype(BF16)
+            value = value * video_scale(live_ref, f + 2, lanes)
+            for k in range(parts):
+                turn[k] = value[:, k * 128 : (k + 1) * 128]
             for v in range(VPG):
-                out_ref[f, v * rows + r] = value[v * cols : (v + 1) * cols]
+                for k in range(parts):
+                    line = [
+                        turn[k, pl.ds(s * VPG + v, blocks, stride=tile)]
+                        for s in range(tile // VPG)
+                    ]
+                    line = jnp.concatenate(line, axis=0).astype(BF16)
+                    out_ref[f, v * rows + r, :, k * 128 : (k + 1) * 128] = line
 
 
 def on_device(
@@ -182,24 +206,31 @@
     row_ids = band * rows - 1 + jnp.arange(rows + 2, dtype=jnp.int32)
     keep = ((row_ids >= 0) & (row_ids < window_rows)).astype(F32)
 
-    own = jnp.take(latent[0], video_of, axis=1)
+    flat = latent[0].reshape(frames, videos, window_rows, local_cols * z)
+    own = jnp.take(flat, video_of, axis=1)
     one = lax.ppermute(own, "tm", [(i, i + 1) for i in range(spans - 1)])
     two = lax.ppermute(own[-1:], "tm", [(i, i + 2) for i in range(spans - 2)])
     line = jnp.concatenate([two, one, own], axis=0)
-    line = jnp.pad(line, ((0, 0), (0, 0), (2, 2), (0, 0), (0, 0)))
+    line = jnp.pad(line, ((0, 0), (0, 0), (2, 2), (0, 0)))
     bands = jnp.stack(
         [line[:, :, b * rows : b * rows + rows + 4] for b in range(BANDS)], axis=0
     )
-    bands = bands.reshape(BANDS, frames + 4, group_count, VPG, rows + 4, local_cols, z)
-    bands = jnp.transpose(bands, (2, 0, 1, 4, 3, 6, 5))
-    bands = bands.reshape(groups, frames + 4, rows + 4, VPG, z, local_cols)
+    bands = bands.reshape(BANDS, frames + 4, group_count, VPG, rows + 4, local_cols * z)
+    bands = jnp.transpose(bands, (2, 0, 1, 4, 3, 5))
+    bands = bands.reshape(groups, frames + 4, rows + 4, VPG, local_cols * z)
     bands = jnp.roll(bands, -(BANDS // 2), axis=0)
     came = lax.all_to_all(bands, "video", split_axis=0, concat_axis=0, tiled=True)
-    came = jnp.transpose(came, (1, 2, 4, 3, 0, 5)).reshape(frames + 4, rows + 4, z, VPG, cols)
+    came = jnp.transpose(came, (1, 2, 0, 3, 4))
     came = (came * live[:, None, None, :, None]).astype(BF16)
-    wide = jnp.pad(came, ((0, 0),) * 4 + ((1, 1),))
-    stacked = jnp.stack([wide[..., k : k + cols] for k in range(3)], axis=2)
-    stacked = stacked.reshape(frames + 4, rows + 4, 3 * z, lanes)
+    behind = jnp.pad(came[:, :, :-1, :, -z:], ((0, 0), (0, 0), (1, 0), (0, 0), (0, 0)))
+    ahead = jnp.pad(came[:, :, 1:, :, :z], ((0, 0), (0, 0), (0, 1), (0, 0), (0, 0)))
+    spare = jnp.zeros(came.shape[:4] + (-(local_cols + 2) * z % 128,), BF16)
+    stacked = jnp.concatenate([behind, came, ahead, spare], axis=-1)
+    tile = groups * VPG
+    stacked = stacked.reshape(frames + 4, rows + 4, tile, -1)
+    taps = jnp.pad(
+        in_weight.reshape(3, 3, 3 * z, width), ((0, 0), (0, 1), (0, 64 - 3 * z), (0, 0))
+    ).reshape(3 * 4 * 64, width)
 
     vmem = pl.BlockSpec(memory_space=pltpu.VMEM)
     smem = pl.BlockSpec(memory_space=pltpu.SMEM)
@@ -213,17 +244,18 @@
     params = pltpu.CompilerParams(vmem_limit_bytes=LIMIT)
     live5 = live[2:]
     hidden, second = pl.pallas_call(
-        front_kernel,
+        functools.partial(front_kernel, z=z),
         out_shape=(
             jax.ShapeDtypeStruct((frames + 2, rows + 2, lanes, width), BF16),
             jax.ShapeDtypeStruct((frames, rows, lanes, width), BF16),
         ),
         in_specs=[smem, smem] + [vmem] * 6 + [hbm],
         out_specs=(vmem, vmem),
-        scratch_shapes=scratch,
+        scratch_shapes=scratch
+        + [pltpu.VMEM((frames + 4, rows + 2, lanes, 256), BF16)],
         compiler_params=params,
     )(
-        live5, keep, stacked, in_weight.reshape(9 * 3 * z, width), in_bias[None],
+        live5, keep, stacked, taps, in_bias[None],
         first_gain[None], first_bias[None], second_gain[None], first_weight,
     )
 
@@ -236,11 +268,11 @@
         tall[:, 0], "video", [((i + 1) % groups, i) for i in range(groups)]
     )
     out = pl.pallas_call(
-        back_kernel,
+        functools.partial(back_kernel, tile=tile),
         out_shape=jax.ShapeDtypeStruct((frames, VPG * rows, cols, width), BF16),
         in_specs=[smem, smem] + [vmem] * 6 + [hbm],
         out_specs=vmem,
-        scratch_shapes=scratch,
+        scratch_shapes=scratch + [pltpu.VMEM((width // 128, lanes, 128), F32)],
         compiler_params=params,
     )(live5, keep, second, behind, above, below, hidden, second_bias[None], second_weight)
     return out[None]

time: 224 us -> 172 us (0.77)
  local copies, waits for them, and re-layouts: 48.6 us -> 13.8 us
  waiting for transfers between devices: 75.1 us -> 61 us
  other arithmetic: 9.76 us -> 5.22 us
    convert_element_type x3 -> x0, local copies, waits for them, and re-layouts: 17.5 us -> none  [on_device(): came = (came * live[:, None, None, :, None]).astype(BF16)]
    ppermute x1, waiting for transfers between devices: 17.3 us -> 4.51 us  [on_device(): two = lax.ppermute(own[-1:], 'tm', [(i, i + 2) for i in range(spans - 2)])]
    unnamed x20 -> x16, local copies, waits for them, and re-layouts: 10.5 us -> 1.4 us
    transpose x1, local copies, waits for them, and re-layouts: 5.74 us -> 0.33 us  [on_device(): bands = jnp.transpose(bands, (2, 0, 1, 4, 3, 5))]
    slice x2, local copies, waits for them, and re-layouts: 3.33 us -> 0.28 us  [on_device(): bands = jnp.roll(bands, -(BANDS // 2), axis=0)]
    convert_element_type x3 -> x1, other arithmetic: 3.07 us -> 0.37 us  [on_device(): came = (came * live[:, None, None, :, None]).astype(BF16)]
  transfers between devices with their start and end apart: 6 -> 6, of which waited for: 4 -> 4; matrix products, arithmetic and copies ran while one was open for 2% -> 4% of each run, Pallas kernels for 0% -> 0%
where the time goes in v1:
time: 172 us
  Pallas kernels  75.8 us (44%)
  waiting for transfers between devices  61 us (35%)
  starting transfers between devices  15.3 us (9%)
  local copies, waits for them, and re-layouts  13.8 us (8%)
  other arithmetic  5.22 us (3%)
    pallas_call x1, Pallas kernels, on_device(): pl.pallas_call(functools.partial(front_kernel, z=z), out_shape=(jax.Shape...  42.7 us
    pallas_call x1, Pallas kernels, on_device(): pl.pallas_call(functools.partial(back_kernel, tile=tile), out_shape=jax.S...  33.1 us
    ppermute x1, waiting for transfers between devices, on_device(): lax.ppermute(second[-2:], 'tm', [(i, i + 1) for i in range(spans - 1)])  28.1 us
    ppermute x1, waiting for transfers between devices, on_device(): lax.ppermute(tall[:, 1], 'video', [(i, (i + 1) % groups) for i in range(g...  20.4 us
    all_to_all x1, waiting for transfers between devices, on_device(): lax.all_to_all(bands, 'video', split_axis=0, concat_axis=0, tiled=True)  8.08 us
    all_to_all x1, starting transfers between devices, on_device(): lax.all_to_all(bands, 'video', split_axis=0, concat_axis=0, tiled=True)  4.88 us
    ppermute x1, waiting for transfers between devices, on_device(): two = lax.ppermute(own[-1:], 'tm', [(i, i + 2) for i in range(spans - 2)])  4.51 us
    ppermute x1, starting transfers between devices, on_device(): lax.ppermute(tall[:, 0], 'video', [((i + 1) % groups, i) for i in range(g...  3.53 us
  transfers between devices with their start and end apart: 6, of which 4 were waited for; matrix products, arithmetic and copies ran while one was open for 4% of the time, Pallas kernels for 0%

profile of v1, /device:TPU:4, one launch (start us, length us, event | category | flops | bytes accessed | tf_op | source)
XLA Modules:
  0.0 171.5 jit_solution(6462260865564876266)
XLA Ops:
  0.0 0.8 select_reduce_fusion
  0.8 1.6 reshape.115
  2.4 0.6 gather_fusion
  3.0 0.1 select_bitcast_fusion
  3.0 3.4 %collective-permute-start.1 = (bf16[3,4,12,256]{3,2,0,1:T(8,128)(2,1)S(1)}, bf16[3,4,12,256]{3,2,0,1:T(8,128)(2,1)S(1)}, u32[]{:S(2)}, u32[]{:S(2)}) collective-permute-start(bf16[3,4,12,256]{3,2,0,1:T(8,128)(2,1)S(1)} %select_bitcast_fusion), channel_id=1, source_target_pairs={{0,8},{8,16},{16,24},{1,9},{9,17},{17,25},{2,10},{10,18},{18,26},{... | collective-permute-start | bytes 221192 | tf_op jit(solution)/shard_map/ppermute | solution.py:211
  6.5 1.3 collective-permute-start
  7.8 4.5 %collective-permute-done = bf16[1,4,12,256]{3,2,0,1:T(8,128)(2,1)S(1)} collective-permute-done((bf16[1,4,12,256]{3,2,0,1:T(8,128)(2,1)S(1)}, bf16[1,4,12,256]{3,2,0,1:T(8,128)(2,1)S(1)}, u32[]{:S(2)}, u32[]{:S(2)}) %collective-permute-start) | collective-permute-done | bytes 24608 | tf_op jit(solution)/shard_map/ppermute | solution.py:212
  12.3 0.1 pad_slice_fusion.3
  12.4 0.1 maximum_bitcast_fusion
  12.6 0.3 copy.40
  12.9 0.0 copy-start.3
  13.0 0.2 slice.69
  13.2 0.1 slice.70
  13.3 1.3 pad_maximum_fusion.1
  14.5 4.9 %all-to-all-start = ((bf16[8,7,7,2,256]{4,3,2,1,0:T(2,128)(2,1)}), bf16[8,7,7,2,256]{4,3,2,1,0:T(2,128)(2,1)S(1)}, u32[]{:S(2)}, u32[]{:S(2)}) async-start(bf16[8,7,7,2,256]{4,3,2,1,0:T(2,128)(2,1)} %pad_maximum_fusion.1), calls=%async_computation | async-start | bytes 802816 | tf_op jit(solution)/shard_map/all_to_all | solution.py:222
  19.4 0.1 dynamic_slice.6
  19.5 0.1 dynamic_slice.7
  19.6 0.1 and_convert_fusion
  19.6 0.6 slice.49.live_ref
  20.2 0.6 broadcast_in_dim.72.in_b_ref
  20.8 0.6 broadcast_in_dim.73.gain1_ref
  21.4 0.6 broadcast_in_dim.74.b1_ref
  22.0 0.5 broadcast_in_dim.75.gain2_ref
  22.6 0.9 pad.19
  23.5 0.1 pad.25.clone
  23.5 0.5 and_convert_fusion.1.keep_ref
  24.0 8.1 %all-to-all-done = bf16[8,7,7,2,256]{4,3,2,1,0:T(2,128)(2,1)S(1)} async-done(((bf16[8,7,7,2,256]{4,3,2,1,0:T(2,128)(2,1)}), bf16[8,7,7,2,256]{4,3,2,1,0:T(2,128)(2,1)S(1)}, u32[]{:S(2)}, u32[]{:S(2)}) %all-to-all-start) | async-done | bytes 401440 | tf_op jit(solution)/shard_map/all_to_all | solution.py:222
  32.1 0.4 fusion.6
  32.5 0.3 fusion.9
  32.8 1.7 %fusion.5 = bf16[7,7,8,2,384]{4,3,1,0,2:T(2,128)(2,1)S(1)} fusion(bf16[7,7,7,2,16]{4,3,1,0,2:T(2,128)(2,1)S(1)} %get-tuple-element.15, bf16[7,7,8,2,256]{4,3,1,0,2:T(2,128)(2,1)S(1)} %fusion.6, bf16[7,7,7,2,16]{4,3,1,0,2:T(2,128)(2,1)S(1)} %get-tuple-element.14, bf16[384]{0:T(512)(128)(2,1)S(1)} %pad.25.clone), kind=kLoop, calls=%fused_computation.12 | loop fusion | flops 4214784 | bytes 1048192 | tf_op jit(solution)/shard_map/concatenate | solution.py:228
  34.6 0.4 copy.41
  35.0 1.0 reshape.105.lat_ref
  36.0 42.7 %shard_map.118 = (bf16[5,5,256,384]{3,2,1,0:T(8,128)(2,1)}, bf16[3,3,256,384]{3,2,1,0:T(8,128)(2,1)}) custom-call(f32[5,2]{1,0:T(8,128)} %slice.49.live_ref, f32[5]{0:T(128)} %and_convert_fusion.1.keep_ref, bf16[7,7,16,384]{3,2,1,0:T(8,128)(2,1)} %reshape.105.lat_ref, bf16[768,384]{1,0:T(8,128)(2,1)} %bitcast.23, f32[1,384]{1,0:T(1,128)} %broadcast_in_dim.72.in_b_ref, ...), custom_call_target="tpu_custom_call" | custom-call | tf_op jit(solution)/shard_map/pallas_call | solution.py:246
  78.7 1.7 copy.42
  80.4 0.1 slice.73
  80.5 2.1 %collective-permute-start.2 = (bf16[2,3,256,384]{3,2,0,1:T(8,128)(2,1)S(1)}, bf16[2,3,256,384]{3,2,0,1:T(8,128)(2,1)S(1)}, u32[]{:S(2)}, u32[]{:S(2)}) collective-permute-start(bf16[2,3,256,384]{3,2,0,1:T(8,128)(2,1)S(1)} %slice.73), channel_id=1, source_target_pairs={{0,8},{8,16},{16,24},{1,9},{9,17},{17,25},{2,10},{10,18},{18,26},{... | collective-permute-start | bytes 3538952 | tf_op jit(solution)/shard_map/ppermute | solution.py:262
  82.6 0.1 slice.61
  82.8 28.1 %collective-permute-done.2 = bf16[2,3,256,384]{3,2,0,1:T(8,128)(2,1)S(1)} collective-permute-done((bf16[2,3,256,384]{3,2,0,1:T(8,128)(2,1)S(1)}, bf16[2,3,256,384]{3,2,0,1:T(8,128)(2,1)S(1)}, u32[]{:S(2)}, u32[]{:S(2)}) %collective-permute-start.2) | collective-permute-done | bytes 1179680 | tf_op jit(solution)/shard_map/ppermute | solution.py:262
  110.8 0.1 slice.60
  110.9 0.2 fusion.2
  111.2 0.1 collective-permute-start.3
  111.2 3.5 %collective-permute-start.4 = (bf16[5,256,384]{2,1,0:T(8,128)(2,1)S(1)}, bf16[5,256,384]{2,1,0:T(8,128)(2,1)S(1)}, u32[]{:S(2)}, u32[]{:S(2)}) collective-permute-start(bf16[5,256,384]{2,1,0:T(8,128)(2,1)S(1)} %get-tuple-element.12), channel_id=1, source_target_pairs={{1,0},{2,1},{3,2},{4,3},{5,4},{6,5},{7,6},{0,7},{9,8},{10,9},{11,1... | collective-permute-start | bytes 2949128 | tf_op jit(solution)/shard_map/ppermute | solution.py:267
  114.8 0.6 broadcast_in_dim.76.b2_ref
  115.3 1.1 copy.44.behind_ref
  116.5 20.4 %collective-permute-done.3.above_ref = bf16[5,256,384]{2,1,0:T(8,128)(2,1)S(1)} collective-permute-done((bf16[5,256,384]{2,1,0:T(8,128)(2,1)S(1)}, bf16[5,256,384]{2,1,0:T(8,128)(2,1)S(1)}, u32[]{:S(2)}, u32[]{:S(2)}) %collective-permute-start.3) | collective-permute-done | bytes 983072 | tf_op jit(solution)/shard_map/ppermute | solution.py:264
  136.9 1.0 copy-done
  137.9 0.3 copy-done.1
  138.2 33.1 %shard_map.119 = bf16[3,6,128,384]{3,2,1,0:T(8,128)(2,1)} custom-call(f32[5,2]{1,0:T(8,128)} %slice.49.live_ref, f32[5]{0:T(128)} %and_convert_fusion.1.keep_ref, bf16[3,3,256,384]{3,2,1,0:T(8,128)(2,1)} %get-tuple-element.7.own_ref, bf16[2,3,256,384]{3,2,1,0:T(8,128)(2,1)} %copy.44.behind_ref, bf16[5,256,384]{2,1,0:T(8,128)(2,1)} %copy-done, ...), custom_call_target="tpu_custom_call" | custom-call | tf_op jit(solution)/shard_map/pallas_call | solution.py:270
  (23 shorter events, 0.1 us)
Async XLA Ops:
  3.0 9.2 %collective-permute-start.1 = (bf16[3,4,12,256]{3,2,0,1:T(8,128)(2,1)S(1)}, bf16[3,4,12,256]{3,2,0,1:T(8,128)(2,1)S(1)}, u32[]{:S(2)}, u32[]{:S(2)}) collective-permute-start(bf16[3,4,12,256]{3,2,0,1:T(8,128)(2,1)S(1)} %select_bitcast_fusion), channel_id=1, source_target_pairs={{0,8},{8,16},{16,24},{1,9},{9,17},{17,25},{2,10},{10,18},{18,26},{... | collective-permute-start | bytes 221192 | tf_op jit(solution)/shard_map/ppermute | solution.py:211
  6.5 5.8 %collective-permute-start = (bf16[1,4,12,256]{3,2,0,1:T(8,128)(2,1)S(1)}, bf16[1,4,12,256]{3,2,0,1:T(8,128)(2,1)S(1)}, u32[]{:S(2)}, u32[]{:S(2)}) collective-permute-start(bf16[1,4,12,256]{3,2,0,1:T(8,128)(2,1)S(1)} %slice.66), channel_id=1, source_target_pairs={{0,16},{8,24},{1,17},{9,25},{2,18},{10,26},{3,19},{11,27},{4,20},{... | collective-permute-start | bytes 73736 | tf_op jit(solution)/shard_map/ppermute | solution.py:212
  12.9 7.3 %copy-start.3 = (f32[384]{0:T(512)S(1)}, f32[384]{0:T(512)}, u32[]{:S(2)}) copy-start(f32[384]{0:T(512)} %param.17) | copy-start | bytes 4612
  12.9 7.9 %copy-start.4 = (f32[384]{0:T(512)S(1)}, f32[384]{0:T(512)}, u32[]{:S(2)}) copy-start(f32[384]{0:T(512)} %param.18) | copy-start | bytes 4612
  12.9 8.5 %copy-start.5 = (f32[384]{0:T(512)S(1)}, f32[384]{0:T(512)}, u32[]{:S(2)}) copy-start(f32[384]{0:T(512)} %param.20) | copy-start | bytes 4612
  12.9 9.1 %copy-start.6 = (f32[384]{0:T(512)S(1)}, f32[384]{0:T(512)}, u32[]{:S(2)}) copy-start(f32[384]{0:T(512)} %param.21) | copy-start | bytes 4612
  12.9 9.6 %copy-start.2 = (bf16[3,3,48,384]{3,2,1,0:T(8,128)(2,1)S(1)}, bf16[3,3,48,384]{3,2,1,0:T(8,128)(2,1)}, u32[]{:S(2)}) copy-start(bf16[3,3,48,384]{3,2,1,0:T(8,128)(2,1)} %param.16) | copy-start | bytes 995332
  14.5 17.6 %all-to-all-start = ((bf16[8,7,7,2,256]{4,3,2,1,0:T(2,128)(2,1)}), bf16[8,7,7,2,256]{4,3,2,1,0:T(2,128)(2,1)S(1)}, u32[]{:S(2)}, u32[]{:S(2)}) async-start(bf16[8,7,7,2,256]{4,3,2,1,0:T(2,128)(2,1)} %pad_maximum_fusion.1), calls=%async_computation | async-start | bytes 802816 | tf_op jit(solution)/shard_map/all_to_all | solution.py:222
  80.5 30.3 %collective-permute-start.2 = (bf16[2,3,256,384]{3,2,0,1:T(8,128)(2,1)S(1)}, bf16[2,3,256,384]{3,2,0,1:T(8,128)(2,1)S(1)}, u32[]{:S(2)}, u32[]{:S(2)}) collective-permute-start(bf16[2,3,256,384]{3,2,0,1:T(8,128)(2,1)S(1)} %slice.73), channel_id=1, source_target_pairs={{0,8},{8,16},{16,24},{1,9},{9,17},{17,25},{2,10},{10,18},{18,26},{... | collective-permute-start | bytes 3538952 | tf_op jit(solution)/shard_map/ppermute | solution.py:262
  110.9 3.8 %copy-start.7 = (f32[384]{0:T(512)S(1)}, f32[384]{0:T(512)}, u32[]{:S(2)}) copy-start(f32[384]{0:T(512)} %param.23) | copy-start | bytes 4612
  111.2 25.7 %collective-permute-start.3 = (bf16[5,256,384]{2,1,0:T(8,128)(2,1)S(1)}, bf16[5,256,384]{2,1,0:T(8,128)(2,1)S(1)}, u32[]{:S(2)}, u32[]{:S(2)}) collective-permute-start(bf16[5,256,384]{2,1,0:T(8,128)(2,1)S(1)} %get-tuple-element.13), channel_id=1, source_target_pairs={{0,1},{1,2},{2,3},{3,4},{4,5},{5,6},{6,7},{7,0},{8,9},{9,10},{10,1... | collective-permute-start | bytes 2949128 | tf_op jit(solution)/shard_map/ppermute | solution.py:264
  111.2 25.7 %collective-permute-start.4 = (bf16[5,256,384]{2,1,0:T(8,128)(2,1)S(1)}, bf16[5,256,384]{2,1,0:T(8,128)(2,1)S(1)}, u32[]{:S(2)}, u32[]{:S(2)}) collective-permute-start(bf16[5,256,384]{2,1,0:T(8,128)(2,1)S(1)} %get-tuple-element.12), channel_id=1, source_target_pairs={{1,0},{2,1},{3,2},{4,3},{5,4},{6,5},{7,6},{0,7},{9,8},{10,9},{11,1... | collective-permute-start | bytes 2949128 | tf_op jit(solution)/shard_map/ppermute | solution.py:267
  136.9 1.1 copy-start
  136.9 1.4 copy-start.1

commit v2 on v1

--- a/solution.py
+++ b/solution.py
@@ -44,23 +44,25 @@
     return half + half * jnp.tanh(half)
 
 
-def accumulate(acc, x, w):
+def accumulate(acc, x, w, outs, ins, part):
     width = acc.shape[-1]
-    rows = acc.shape[1]
-    frames = acc.shape[0]
-
-    def step(j, carry):
-        for a in range(frames + 2):
-            low, high = max(0, a - frames + 1), min(2, a)
-            lhs = x[a, pl.ds(j, 3)].reshape(rows, 3 * width)
+    lanes = x.shape[2]
+    steps, (tap, tap_by), (row, row_by), count = part
+
+    def step(t, carry):
+        j, first = tap + t * tap_by, row + t * row_by
+        cells = pl.ds(pl.multiple_of((first - j) * lanes, lanes), count * lanes)
+        for a in ins:
+            low, high = max(0, a - outs[-1]), min(2, a - outs[0])
+            lhs = x[a, pl.ds(first, count)].reshape(count * lanes, 3 * width)
             res = jnp.dot(
                 lhs, w[j, :, low * width : (high + 1) * width], preferred_element_type=F32
             )
             for i in range(low, high + 1):
-                acc[a - i] += res[:, (i - low) * width : (i - low + 1) * width]
+                acc[a - i, cells] += res[:, (i - low) * width : (i - low + 1) * width]
         return carry
 
-    lax.fori_loop(0, 3, step, 0)
+    lax.fori_loop(0, steps, step, 0)
 
 
 def video_scale(mask_ref, frame, lanes):
@@ -85,95 +87,193 @@
     lax.fori_loop(0, lat_ref.shape[0], frame, 0)
 
 
-def front_kernel(
-    live_ref, keep_ref, lat_ref, in_w_ref, in_b_ref, gain1_ref, b1_ref, gain2_ref, w1_ref,
-    hidden_ref, second_ref, x, w, acc, sems, q, *, z,
+def block_kernel(
+    live_ref, keep_ref, lat_ref, in_w_ref, in_b_ref, gain1_ref, b1_ref, gain2_ref, b2_ref,
+    w1_ref, w2_ref, out_ref,
+    x, w1, w2, acc, q, hidden, second, behind, above, below, turn,
+    w1_sems, w2_sems, send_sems, recv_sems, *, z, spans, groups,
 ):
-    copies = weight_copies(w1_ref, w, sems)
-    for copy in copies:
+    span, place = lax.axis_index("tm"), lax.axis_index("video")
+    band = (place + BANDS // 2) % groups % BANDS
+    up, down = (place + 1) % groups, (place + groups - 1) % groups
+    first, last = span == 0, span == spans - 1
+    top, bottom = band == 0, band == BANDS - 1
+    ways = [
+        (jnp.logical_not(first), {"tm": span - 1}),
+        (jnp.logical_not(last), {"tm": span + 1}),
+        (jnp.logical_not(top), {"video": down}),
+        (jnp.logical_not(bottom), {"video": up}),
+    ]
+    barrier = pltpu.get_barrier_semaphore()
+    for there, device in ways:
+        @pl.when(there)
+        def _(device=device):
+            pl.semaphore_signal(
+                barrier, inc=1, device_id=device, device_id_type=pl.DeviceIdType.MESH
+            )
+
+    loads = weight_copies(w1_ref, w1, w1_sems)
+    more_loads = weight_copies(w2_ref, w2, w2_sems)
+    for copy in loads:
         copy.start()
-    frames, rows, lanes = x.shape[:3]
-    tile = lat_ref.shape[2]
+    frames, rows = second.shape[:2]
+    lanes, tile = x.shape[2], lat_ref.shape[2]
+
+    def remote(source, target, k, device):
+        return pltpu.make_async_remote_copy(
+            src_ref=source, dst_ref=target, send_sem=send_sems.at[k], recv_sem=recv_sems.at[k],
+            device_id=device, device_id_type=pl.DeviceIdType.MESH,
+        )
+
+    late, early = pl.ds(frames - 2, 2), pl.ds(0, frames - 2)
+    back = remote(second.at[late], behind, 0, {"tm": span + 1})
+    to_up = [
+        remote(second.at[late, rows - 1], above.at[pl.ds(frames, 2)], 1, {"video": up}),
+        remote(second.at[early, rows - 1], above.at[pl.ds(2, frames - 2)], 2, {"video": up}),
+        remote(behind.at[:, rows - 1], above.at[pl.ds(0, 2)], 3, {"video": up}),
+    ]
+    to_down = [
+        remote(second.at[late, 0], below.at[pl.ds(frames, 2)], 4, {"video": down}),
+        remote(second.at[early, 0], below.at[pl.ds(2, frames - 2)], 5, {"video": down}),
+        remote(behind.at[:, 0], below.at[pl.ds(0, 2)], 6, {"video": down}),
+    ]
+
+    def send_rows(k):
+        @pl.when(jnp.logical_not(bottom))
+        def _():
+            to_up[k].start()
+
+        @pl.when(jnp.logical_not(top))
+        def _():
+            to_down[k].start()
+
     gather_taps(lat_ref, q, z, lanes // tile)
 
     def cell(index, carry):
-        f, r = index // rows, index % rows
+        f, r = index // (rows + 2), index % (rows + 2)
         taps = jnp.concatenate([q[f + i, r] for i in range(3)], axis=1)
         value = jnp.dot(taps, in_w_ref[...], preferred_element_type=F32)
         scale = video_scale(live_ref, f, lanes) * keep_ref[r]
         value = ((value + in_b_ref[...]) * scale).astype(BF16)
-        hidden_ref[f, r] = value
+        hidden[f, r] = value
         spread_columns(x.at[f, r], norm_silu(value.astype(F32), gain1_ref[...]), tile)
         return carry
 
-    lax.fori_loop(0, frames * rows, cell, 0)
-    for o in range(acc.shape[0]):
+    lax.fori_loop(0, (frames + 2) * (rows + 2), cell, 0)
+    for o in range(frames):
         acc[o] = jnp.broadcast_to(b1_ref[...], acc.shape[1:])
-    for copy in copies:
+    for copy in loads:
         copy.wait()
-    accumulate(acc, x, w)
-
-    def finish(index, carry):
-        f, r = index // (rows - 2), index % (rows - 2)
-        value = acc[f, pl.ds(pl.multiple_of(r * lanes, lanes), lanes)]
-        value = value * video_scale(live_ref, f + 2, lanes)
-        second_ref[f, r] = norm_silu(value, gain2_ref[...]).astype(BF16)
-        return carry
-
-    lax.fori_loop(0, acc.shape[0] * (rows - 2), finish, 0)
-
-
-def back_kernel(
-    live_ref, keep_ref, own_ref, behind_ref, above_ref, below_ref, hidden_ref, b2_ref, w2_ref,
-    out_ref, x, w, acc, sems, turn, *, tile,
-):
-    frames, rows, lanes, width = own_ref.shape
-    copies = weight_copies(w2_ref, w, sems)
-    for copy in copies:
+    for copy in more_loads:
         copy.start()
-
-    def fill_own(index, carry):
-        f, r = index // rows, index % rows
-        spread_columns(x.at[f + 2, r + 1], own_ref[f, r].astype(F32), tile)
-        return carry
-
-    lax.fori_loop(0, frames * rows, fill_own, 0)
-
-    def fill_behind(index, carry):
-        f, r = index // rows, index % rows
-        spread_columns(x.at[f, r + 1], behind_ref[f, r].astype(F32), tile)
-        return carry
-
-    lax.fori_loop(0, 2 * rows, fill_behind, 0)
-
-    def fill_rows(f, carry):
-        spread_columns(x.at[f, 0], above_ref[f].astype(F32) * keep_ref[0], tile)
-        spread_columns(x.at[f, rows + 1], below_ref[f].astype(F32) * keep_ref[rows + 1], tile)
-        return carry
-
-    lax.fori_loop(0, frames + 2, fill_rows, 0)
+    whole = (3, (0, 1), (0, 1), rows)
+
+    def finish(f):
+        def row(r, carry):
+            value = acc[f, pl.ds(pl.multiple_of(r * lanes, lanes), lanes)]
+            value = value * video_scale(live_ref, f + 2, lanes)
+            second[f, r] = norm_silu(value, gain2_ref[...]).astype(BF16)
+            return carry
+
+        lax.fori_loop(0, rows, row, 0)
+
+    accumulate(acc, x, w1, range(frames - 2, frames), range(frames - 2, frames + 2), whole)
+    for f in range(frames - 2, frames):
+        finish(f)
+    pl.semaphore_wait(barrier, sum(jnp.where(there, 1, 0) for there, _ in ways))
+
+    @pl.when(jnp.logical_not(last))
+    def _():
+        back.start()
+
+    send_rows(0)
+    accumulate(acc, x, w1, range(0, frames - 2), range(0, frames), whole)
+    for f in range(frames - 2):
+        finish(f)
+    send_rows(1)
+
+    def fill(source, at_frame, at_row, count):
+        def one(index, carry):
+            f, r = index // rows, index % rows
+            spread_columns(x.at[f + at_frame, r + at_row], source[f, r].astype(F32), tile)
+            return carry
+
+        lax.fori_loop(0, count * rows, one, 0)
+
+    def fill_edges(start, count, ks):
+        for source, empty, copies, at_row in (
+            (above, top, to_up, 0), (below, bottom, to_down, rows + 1)
+        ):
+            @pl.when(jnp.logical_not(empty))
+            def _(source=source, copies=copies, at_row=at_row):
+                for k in ks:
+                    copies[k].wait_recv()
+
+                def one(f, carry):
+                    spread_columns(x.at[f, at_row], source[f].astype(F32), tile)
+                    return carry
+
+                lax.fori_loop(start, start + count, one, 0)
+
+            @pl.when(empty)
+            def _(at_row=at_row):
+                for f in range(start, start + count):
+                    x[f, at_row] = jnp.zeros(x.shape[2:], BF16)
+
+    fill(second, 2, 1, frames)
     for o in range(frames):
         acc[o] = jnp.broadcast_to(b2_ref[...], acc.shape[1:])
-    for copy in copies:
+    for copy in more_loads:
         copy.wait()
-    accumulate(acc, x, w)
+    own_frames, every = range(2, frames + 2), range(frames)
+    middle = (1, (1, 0), (1, 0), rows)
+    beside = (2, (0, 2), (1, 1), rows - 1)
+    outer = (2, (0, 2), (0, rows + 1), 1)
+    accumulate(acc, x, w2, every, own_frames, middle)
+    accumulate(acc, x, w2, every, own_frames, beside)
+    fill_edges(2, frames, (0, 1))
+    accumulate(acc, x, w2, every, own_frames, outer)
+
+    @pl.when(jnp.logical_not(first))
+    def _():
+        back.wait_recv()
+
+    @pl.when(first)
+    def _():
+        behind[...] = jnp.zeros(behind.shape, BF16)
+
+    send_rows(2)
+    fill(behind, 0, 1, 2)
+    accumulate(acc, x, w2, every, range(2), middle)
+    accumulate(acc, x, w2, every, range(2), beside)
+    fill_edges(0, 2, (2,))
+    accumulate(acc, x, w2, every, range(2), outer)
 
     blocks = lanes // tile
-    parts = width // 128
     for f in range(frames):
         for r in range(rows):
-            value = acc[f, r * lanes : (r + 1) * lanes] + hidden_ref[f + 2, r + 1].astype(F32)
+            value = acc[f, r * lanes : (r + 1) * lanes] + hidden[f + 2, r + 1].astype(F32)
             value = value * video_scale(live_ref, f + 2, lanes)
-            for k in range(parts):
+            for k in range(turn.shape[0]):
                 turn[k] = value[:, k * 128 : (k + 1) * 128]
             for v in range(VPG):
-                for k in range(parts):
+                for k in range(turn.shape[0]):
                     line = [
                         turn[k, pl.ds(s * VPG + v, blocks, stride=tile)]
                         for s in range(tile // VPG)
                     ]
                     line = jnp.concatenate(line, axis=0).astype(BF16)
                     out_ref[f, v * rows + r, :, k * 128 : (k + 1) * 128] = line
+
+    @pl.when(jnp.logical_not(last))
+    def _():
+        back.wait_send()
+
+    for copies, empty in ((to_up, bottom), (to_down, top)):
+        @pl.when(jnp.logical_not(empty))
+        def _(copies=copies):
+            for copy in copies:
+                copy.wait_send()
 
 
 def on_device(
@@ -238,43 +338,33 @@
     scratch = [
         pltpu.VMEM((frames + 2, rows + 2, lanes, 3 * width), BF16),
         pltpu.VMEM((3, 3 * width, 3 * width), BF16),
+        pltpu.VMEM((3, 3 * width, 3 * width), BF16),
         pltpu.VMEM((frames, rows * lanes, width), F32),
+        pltpu.VMEM((frames + 4, rows + 2, lanes, 256), BF16),
+        pltpu.VMEM((frames + 2, rows + 2, lanes, width), BF16),
+        pltpu.VMEM((frames, rows, lanes, width), BF16),
+        pltpu.VMEM((2, rows, lanes, width), BF16),
+        pltpu.VMEM((frames + 2, lanes, width), BF16),
+        pltpu.VMEM((frames + 2, lanes, width), BF16),
+        pltpu.VMEM((width // 128, lanes, 128), F32),
         pltpu.SemaphoreType.DMA((3, 3)),
-    ]
-    params = pltpu.CompilerParams(vmem_limit_bytes=LIMIT)
-    live5 = live[2:]
-    hidden, second = pl.pallas_call(
-        functools.partial(front_kernel, z=z),
-        out_shape=(
-            jax.ShapeDtypeStruct((frames + 2, rows + 2, lanes, width), BF16),
-            jax.ShapeDtypeStruct((frames, rows, lanes, width), BF16),
+        pltpu.SemaphoreType.DMA((3, 3)),
+        pltpu.SemaphoreType.DMA((7,)),
+        pltpu.SemaphoreType.DMA((7,)),
+    ]
+    out = pl.pallas_call(
+        functools.partial(block_kernel, z=z, spans=spans, groups=groups),
+        out_shape=jax.ShapeDtypeStruct((frames, VPG * rows, cols, width), BF16),
+        in_specs=[smem, smem] + [vmem] * 7 + [hbm] * 2,
+        out_specs=vmem,
+        scratch_shapes=scratch,
+        compiler_params=pltpu.CompilerParams(
+            vmem_limit_bytes=LIMIT, collective_id=0, has_side_effects=True
         ),
-        in_specs=[smem, smem] + [vmem] * 6 + [hbm],
-        out_specs=(vmem, vmem),
-        scratch_shapes=scratch
-        + [pltpu.VMEM((frames + 4, rows + 2, lanes, 256), BF16)],
-        compiler_params=params,
     )(
-        live5, keep, stacked, taps, in_bias[None],
-        first_gain[None], first_bias[None], second_gain[None], first_weight,
+        live[2:], keep, stacked, taps, in_bias[None], first_gain[None], first_bias[None],
+        second_gain[None], second_bias[None], first_weight, second_weight,
     )
-
-    behind = lax.ppermute(second[-2:], "tm", [(i, i + 1) for i in range(spans - 1)])
-    tall = jnp.concatenate([behind[:, 0::rows - 1], second[:, 0::rows - 1]], axis=0)
-    above = lax.ppermute(
-        tall[:, 1], "video", [(i, (i + 1) % groups) for i in range(groups)]
-    )
-    below = lax.ppermute(
-        tall[:, 0], "video", [((i + 1) % groups, i) for i in range(groups)]
-    )
-    out = pl.pallas_call(
-        functools.partial(back_kernel, tile=tile),
-        out_shape=jax.ShapeDtypeStruct((frames, VPG * rows, cols, width), BF16),
-        in_specs=[smem, smem] + [vmem] * 6 + [hbm],
-        out_specs=vmem,
-        scratch_shapes=scratch + [pltpu.VMEM((width // 128, lanes, 128), F32)],
-        compiler_params=params,
-    )(live5, keep, second, behind, above, below, hidden, second_bias[None], second_weight)
     return out[None]
 
 

time: 172 us -> 112 us (0.65)
  waiting for transfers between devices: 61 us -> 12 us
  starting transfers between devices: 15.3 us -> 9.56 us
  Pallas kernels: 75.8 us -> 71.4 us
    ppermute x3 -> x0, waiting for transfers between devices: 48.5 us -> none  [the longest x1 28.1 us: on_device(): lax.ppermute(second[-2:], 'tm', [(i, i + 1) for i in range(spans - 1)])]
    ppermute x3 -> x0, starting transfers between devices: 5.69 us -> none  [the longest x1 3.53 us: on_device(): lax.ppermute(tall[:, 0], 'video', [((i + 1) % groups, i) for i in range(g...]
    pallas_call x2 -> x1, Pallas kernels: 75.8 us -> 71.4 us  [on_device(): pl.pallas_call(functools.partial(block_kernel, z=z, spans=spans, groups=g...]
  transfers between devices with their start and end apart: 6 -> 3, of which waited for: 4 -> 2; matrix products, arithmetic and copies ran while one was open for 4% -> 5% of each run, Pallas kernels for 0% -> 0%
where the time goes in v2:
time: 112 us; the launch traced here: 110 us
  Pallas kernels  71.4 us (64%)
  local copies, waits for them, and re-layouts  12.2 us (11%)
  waiting for transfers between devices  12 us (11%)
  starting transfers between devices  9.56 us (9%)
  other arithmetic  5.02 us (4%)
    pallas_call x1, Pallas kernels, on_device(): pl.pallas_call(functools.partial(block_kernel, z=z, spans=spans, groups=g...  71.4 us
    all_to_all x1, waiting for transfers between devices, on_device(): lax.all_to_all(bands, 'video', split_axis=0, concat_axis=0, tiled=True)  7.46 us
    all_to_all x1, starting transfers between devices, on_device(): lax.all_to_all(bands, 'video', split_axis=0, concat_axis=0, tiled=True)  4.88 us
    ppermute x1, waiting for transfers between devices, on_device(): two = lax.ppermute(own[-1:], 'tm', [(i, i + 2) for i in range(spans - 2)])  4.51 us
    ppermute x1, starting transfers between devices, on_device(): one = lax.ppermute(own, 'tm', [(i, i + 1) for i in range(spans - 1)])  3.39 us
    unnamed x13, local copies, waits for them, and re-layouts  2.97 us
  transfers between devices with their start and end apart: 3, of which 2 were waited for; matrix products, arithmetic and copies ran while one was open for 5% of the time, Pallas kernels for 0%

profile of v2, /device:TPU:4, one launch (start us, length us, event | category | flops | bytes accessed | tf_op | source)
XLA Modules:
  0.0 110.3 jit_solution(6597400684254425666)
XLA Ops:
  0.0 0.8 select_reduce_fusion
  0.8 1.6 %reshape.115 = bf16[3,4,12,256]{3,2,1,0:T(8,128)(2,1)S(1)} reshape(bf16[1,3,4,12,16,16]{5,4,3,2,1,0:T(8,128)(2,1)} %param.12) | data formatting | bytes 147456 | tf_op jit(solution)/shard_map/reshape;squeeze | solution.py:309
  2.4 0.6 gather_fusion
  3.0 0.1 select_bitcast_fusion
  3.0 3.4 %collective-permute-start.1 = (bf16[3,4,12,256]{3,2,0,1:T(8,128)(2,1)S(1)}, bf16[3,4,12,256]{3,2,0,1:T(8,128)(2,1)S(1)}, u32[]{:S(2)}, u32[]{:S(2)}) collective-permute-start(bf16[3,4,12,256]{3,2,0,1:T(8,128)(2,1)S(1)} %select_bitcast_fusion), channel_id=1, source_target_pairs={{0,8},{8,16},{16,24},{1,9},{9,17},{17,25},{2,10},{10,18},{18,26},{... | collective-permute-start | bytes 221192 | tf_op jit(solution)/shard_map/ppermute | solution.py:311
  6.5 1.3 %collective-permute-start = (bf16[1,4,12,256]{3,2,0,1:T(8,128)(2,1)S(1)}, bf16[1,4,12,256]{3,2,0,1:T(8,128)(2,1)S(1)}, u32[]{:S(2)}, u32[]{:S(2)}) collective-permute-start(bf16[1,4,12,256]{3,2,0,1:T(8,128)(2,1)S(1)} %slice.46), channel_id=1, source_target_pairs={{0,16},{8,24},{1,17},{9,25},{2,18},{10,26},{3,19},{11,27},{4,20},{... | collective-permute-start | bytes 73736 | tf_op jit(solution)/shard_map/ppermute | solution.py:312
  7.8 4.5 %collective-permute-done = bf16[1,4,12,256]{3,2,0,1:T(8,128)(2,1)S(1)} collective-permute-done((bf16[1,4,12,256]{3,2,0,1:T(8,128)(2,1)S(1)}, bf16[1,4,12,256]{3,2,0,1:T(8,128)(2,1)S(1)}, u32[]{:S(2)}, u32[]{:S(2)}) %collective-permute-start) | collective-permute-done | bytes 24608 | tf_op jit(solution)/shard_map/ppermute | solution.py:312
  12.3 0.0 collective-permute-done.1
  12.3 0.1 pad_slice_fusion.1
  12.4 0.1 maximum_bitcast_fusion
  12.6 0.3 copy.28
  12.9 0.0 copy-start.1
  12.9 0.0 copy-start.2
  12.9 0.0 copy-start.3
  12.9 0.0 copy-start.4
  12.9 0.0 copy-start.5
  13.0 0.1 slice.50
  13.0 0.0 copy-start
  13.0 0.2 slice.49
  13.3 1.3 %pad_maximum_fusion = bf16[8,7,7,2,256]{4,3,2,1,0:T(2,128)(2,1)} fusion(bf16[2,7,7,2,256]{4,3,2,1,0:T(2,128)(2,1)S(1)} %slice.50, bf16[6,7,7,2,256]{4,3,2,1,0:T(2,128)(2,1)S(1)} %slice.49), kind=kLoop, calls=%fused_computation.9 | loop fusion | flops 200704 | bytes 802816 | tf_op jit(solution)/shard_map/jit(_roll_static)/concatenate | solution.py:321
  14.5 4.9 %all-to-all-start = ((bf16[8,7,7,2,256]{4,3,2,1,0:T(2,128)(2,1)}), bf16[8,7,7,2,256]{4,3,2,1,0:T(2,128)(2,1)S(1)}, u32[]{:S(2)}, u32[]{:S(2)}) async-start(bf16[8,7,7,2,256]{4,3,2,1,0:T(2,128)(2,1)} %pad_maximum_fusion), calls=%async_computation | async-start | bytes 802816 | tf_op jit(solution)/shard_map/all_to_all | solution.py:322
  19.4 0.0 copy-done.1
  19.4 0.6 broadcast_in_dim.72.in_b_ref
  20.0 0.0 copy-done.2
  20.0 0.6 broadcast_in_dim.73.gain1_ref
  20.6 0.0 copy-done.3
  20.6 0.6 broadcast_in_dim.74.b1_ref
  21.1 0.0 copy-done.4
  21.1 0.6 broadcast_in_dim.75.gain2_ref
  21.7 0.0 copy-done.5
  21.7 0.6 broadcast_in_dim.76.b2_ref
  22.3 0.1 dynamic_slice.6
  22.4 0.1 dynamic_slice.7
  22.5 0.1 and_convert_fusion
  22.6 0.6 slice.34.live_ref
  23.2 0.0 copy-done
  23.2 0.9 pad.19
  24.1 0.1 pad.23.clone
  24.1 0.5 and_convert_fusion.1.keep_ref
  24.7 7.5 %all-to-all-done = bf16[8,7,7,2,256]{4,3,2,1,0:T(2,128)(2,1)S(1)} async-done(((bf16[8,7,7,2,256]{4,3,2,1,0:T(2,128)(2,1)}), bf16[8,7,7,2,256]{4,3,2,1,0:T(2,128)(2,1)S(1)}, u32[]{:S(2)}, u32[]{:S(2)}) %all-to-all-start) | async-done | bytes 401440 | tf_op jit(solution)/shard_map/all_to_all | solution.py:322
  32.1 0.4 fusion.3
  32.5 0.3 fusion.6
  32.8 1.7 %fusion.2 = bf16[7,7,8,2,384]{4,3,1,0,2:T(2,128)(2,1)S(1)} fusion(bf16[7,7,7,2,16]{4,3,1,0,2:T(2,128)(2,1)S(1)} %get-tuple-element.9, bf16[7,7,8,2,256]{4,3,1,0,2:T(2,128)(2,1)S(1)} %fusion.3, bf16[7,7,7,2,16]{4,3,1,0,2:T(2,128)(2,1)S(1)} %get-tuple-element.8, bf16[384]{0:T(512)(128)(2,1)S(1)} %pad.23.clone), kind=kLoop, calls=%fused_computation.6 | loop fusion | flops 4214784 | bytes 1048192 | tf_op jit(solution)/shard_map/concatenate | solution.py:328
  34.6 0.4 copy.29
  35.0 1.0 reshape.105.lat_ref
  36.0 71.4 %shard_map.118 = bf16[3,6,128,384]{3,2,1,0:T(8,128)(2,1)} custom-call(f32[5,2]{1,0:T(8,128)} %slice.34.live_ref, f32[5]{0:T(128)} %and_convert_fusion.1.keep_ref, bf16[7,7,16,384]{3,2,1,0:T(8,128)(2,1)} %reshape.105.lat_ref, bf16[768,384]{1,0:T(8,128)(2,1)} %bitcast.20, f32[1,384]{1,0:T(1,128)} %broadcast_in_dim.72.in_b_ref, ...), custom_call_target="tpu_custom_call" | custom-call | tf_op jit(solution)/shard_map/pallas_call | solution.py:355
  107.4 2.9 %copy.32 = bf16[1,3,6,128,384]{4,3,2,1,0:T(8,128)(2,1)} copy(bf16[1,3,6,128,384]{4,3,2,1,0:T(8,128)(2,1)} %bitcast.19) | data formatting | bytes 3538944
  (8 shorter events, 0.1 us)
Async XLA Ops:
  3.0 9.2 %collective-permute-start.1 = (bf16[3,4,12,256]{3,2,0,1:T(8,128)(2,1)S(1)}, bf16[3,4,12,256]{3,2,0,1:T(8,128)(2,1)S(1)}, u32[]{:S(2)}, u32[]{:S(2)}) collective-permute-start(bf16[3,4,12,256]{3,2,0,1:T(8,128)(2,1)S(1)} %select_bitcast_fusion), channel_id=1, source_target_pairs={{0,8},{8,16},{16,24},{1,9},{9,17},{17,25},{2,10},{10,18},{18,26},{... | collective-permute-start | bytes 221192 | tf_op jit(solution)/shard_map/ppermute | solution.py:311
  6.5 5.8 %collective-permute-start = (bf16[1,4,12,256]{3,2,0,1:T(8,128)(2,1)S(1)}, bf16[1,4,12,256]{3,2,0,1:T(8,128)(2,1)S(1)}, u32[]{:S(2)}, u32[]{:S(2)}) collective-permute-start(bf16[1,4,12,256]{3,2,0,1:T(8,128)(2,1)S(1)} %slice.46), channel_id=1, source_target_pairs={{0,16},{8,24},{1,17},{9,25},{2,18},{10,26},{3,19},{11,27},{4,20},{... | collective-permute-start | bytes 73736 | tf_op jit(solution)/shard_map/ppermute | solution.py:312
  12.9 6.5 %copy-start.1 = (f32[384]{0:T(512)S(1)}, f32[384]{0:T(512)}, u32[]{:S(2)}) copy-start(f32[384]{0:T(512)} %param.17) | copy-start | bytes 4612
  12.9 7.1 %copy-start.2 = (f32[384]{0:T(512)S(1)}, f32[384]{0:T(512)}, u32[]{:S(2)}) copy-start(f32[384]{0:T(512)} %param.18) | copy-start | bytes 4612
  12.9 7.6 %copy-start.3 = (f32[384]{0:T(512)S(1)}, f32[384]{0:T(512)}, u32[]{:S(2)}) copy-start(f32[384]{0:T(512)} %param.20) | copy-start | bytes 4612
  12.9 8.2 %copy-start.4 = (f32[384]{0:T(512)S(1)}, f32[384]{0:T(512)}, u32[]{:S(2)}) copy-start(f32[384]{0:T(512)} %param.21) | copy-start | bytes 4612
  12.9 8.8 %copy-start.5 = (f32[384]{0:T(512)S(1)}, f32[384]{0:T(512)}, u32[]{:S(2)}) copy-start(f32[384]{0:T(512)} %param.23) | copy-start | bytes 4612
  13.0 10.1 %copy-start = (bf16[3,3,48,384]{3,2,1,0:T(8,128)(2,1)S(1)}, bf16[3,3,48,384]{3,2,1,0:T(8,128)(2,1)}, u32[]{:S(2)}) copy-start(bf16[3,3,48,384]{3,2,1,0:T(8,128)(2,1)} %param.16) | copy-start | bytes 995332
  14.5 17.6 %all-to-all-start = ((bf16[8,7,7,2,256]{4,3,2,1,0:T(2,128)(2,1)}), bf16[8,7,7,2,256]{4,3,2,1,0:T(2,128)(2,1)S(1)}, u32[]{:S(2)}, u32[]{:S(2)}) async-start(bf16[8,7,7,2,256]{4,3,2,1,0:T(2,128)(2,1)} %pad_maximum_fusion), calls=%async_computation | async-start | bytes 802816 | tf_op jit(solution)/shard_map/all_to_all | solution.py:322
